TPU v7x, 256 devices: a whole 4x4x8 slice. The times are simulated.
256 devices in a mesh: band: 32 (over z, x), gvec: 8 (over y, core).
Axes of the slice: x: 4, y: 4, z: 8, core: 2. Of those that a mesh axis runs over, the one named last changes fastest.
Arguments:
- pairs: bfloat16 [32, 8, 512, 640], P(None, 'gvec', 'band'), may hold values from -0.59765625 to 0.59765625
- cond_energy: float32 [512], replicated, may hold values from 0.5 to 12
- val_energy: float32 [32, 8], replicated, may hold values from -12 to -2
- band_counts: int32 [32], replicated, may hold values from 1 to 16, as said below
- slab: int32 [1], replicated, may hold values from 0 to 31
Outputs:
- chi_zero: float32 [20480, 20480], P('gvec', 'band')
Inputs may be any that keep to these rules, and one draw needn't show every extreme that they name: `band_counts`: every owner has at least one occupied slot, and in every draw some owner has all 16 slots occupied.
All inputs are finite; a program needn't handle non-finite values.
Results may differ from a plain program's by a relative error of at most 0.0028.
Values may be sent and summed in bfloat16 or wider, within the bound.
No kernel may reach another device: no remote copies, remote signals or barrier semaphores. Data moves between devices by JAX's collectives and lax.ppermute only.
A program may use at most 128 MiB of HBM per device.

v0:
```python
import jax
import jax.numpy as jnp
from jax import lax
from jax.sharding import PartitionSpec as P


def on_device(pairs, cond_energy, val_energy, band_counts, slab):
    n_band = lax.axis_size("band")
    n_gvec = lax.axis_size("gvec")
    ratio = n_band // n_gvec
    local_v = pairs.shape[1]
    slot_count = pairs.shape[2]
    col_width = pairs.shape[3]
    energies = lax.dynamic_index_in_dim(val_energy, slab[0], 0, keepdims=False)
    slots = jnp.arange(slot_count, dtype=jnp.int32)
    live = (slots[None, :] < band_counts[:, None]).reshape(-1)
    weight = jnp.where(
        live[None, :], 2.0 / (energies[:, None] - cond_energy[None, :]), jnp.float32(0.0)
    )
    blocked = pairs.reshape(n_gvec, ratio, local_v, slot_count, col_width)
    by_block = lax.all_to_all(blocked, "gvec", split_axis=0, concat_axis=2, tiled=True)
    rows_all = lax.all_gather(by_block, "band", axis=3, tiled=True)[0]
    by_column = lax.all_to_all(pairs, "band", split_axis=0, concat_axis=2, tiled=True)
    cols_all = lax.all_gather(by_column, "gvec", axis=1, tiled=True)[0]
    scaled = (weight[:, :, None] * cols_all.astype(jnp.float32)).astype(jnp.bfloat16)
    result = lax.dot_general(
        rows_all, scaled, (((1, 2), (0, 1)), ((), ())), preferred_element_type=jnp.float32
    )
    return result.reshape(ratio * col_width, col_width)


def solution(mesh):
    in_specs = (P(None, "gvec", "band", None), P(), P(), P(), P())
    out_specs = P("gvec", "band")
    return jax.shard_map(
        on_device, mesh=mesh, in_specs=in_specs, out_specs=out_specs, check_vma=False
    )
```

profile of v0, /device:TPU:1, one launch (start us, length us, event | category | flops | bytes accessed | tf_op | source)
XLA Modules:
  0.0 263.4 jit_solution(6837848196494836438)
XLA Ops:
  6.5 0.0 copy-start
  6.5 0.0 all-gather.6.cloned.1.call-start
  6.5 17.7 %all_to_all.30 = bf16[8,4,1,16,640]{4,3,2,1,0:T(8,128)(2,1)S(1)} all-to-all(bf16[8,4,1,16,640]{4,3,2,1,0:T(8,128)(2,1)} %bitcast.24), channel_id=1, replica_groups=mesh['band'=32,'gvec'=8] {'gvec'}, dimensions={0} | all-to-all | bytes 1310720 | tf_op jit(solution)/shard_map/all_to_all | solution.py:21
  24.3 1.2 copy.8
  25.5 0.0 all-gather.6.cloned.1.call-update
  25.5 0.0 all-gather.4.cloned.1.call-start
  25.6 32.6 %all_to_all.31 = bf16[32,1,16,640]{3,2,1,0:T(8,128)(2,1)} all-to-all(bf16[32,1,16,640]{3,2,1,0:T(8,128)(2,1)} %param.5), channel_id=1, replica_groups=mesh['band'=32,'gvec'=8] {'band'}, dimensions={0} | all-to-all | bytes 1310720 | tf_op jit(solution)/shard_map/all_to_all | solution.py:23
  58.2 0.0 all-gather.4.cloned.1.call-update
  58.8 0.7 iota_compare_fusion
  59.6 0.1 lt.27
  59.7 0.0 copy-done
  59.7 0.2 dynamic-slice_reduce_fusion
  59.8 0.8 divide_select_fusion
  60.6 133.8 %all-gather.6.cloned.1.call-done = bf16[1,4,8,1,512,640]{5,2,3,1,0,4:T(8,128)(2,1)} async-done(((bf16[1,4,8,1,16,640]{5,2,3,1,0,4:T(8,128)(2,1)}), bf16[1,4,8,1,512,640]{5,2,3,1,0,4:T(8,128)(2,1)}) %all-gather.6.cloned.1.call-update) | async-done | bytes 20971536 | tf_op jit(solution)/shard_map/all_gather | solution.py:22
  194.4 30.2 %copy.9 = bf16[1,4,8,1,512,640]{4,5,2,1,3,0:T(8,128)(2,1)} copy(bf16[1,4,8,1,512,640]{5,2,3,1,0,4:T(8,128)(2,1)} %all-gather.6.cloned.1.call-done) | data formatting | bytes 41943040 | tf_op jit(solution)/shard_map/all_gather | solution.py:22
  224.6 8.6 %all-gather.4.cloned.1.call-done = bf16[1,8,512,640]{3,2,0,1:T(8,128)(2,1)} async-done(((bf16[1,1,512,640]{3,2,0,1:T(8,128)(2,1)}), bf16[1,8,512,640]{3,2,0,1:T(8,128)(2,1)}) %all-gather.4.cloned.1.call-update) | async-done | bytes 5242896 | tf_op jit(solution)/shard_map/all_gather | solution.py:24
  233.3 23.3 %fusion = f32[640,4,640,1]{0,2,3,1:T(8,128)} fusion(bf16[1,4,8,1,512,640]{4,5,2,1,3,0:T(8,128)(2,1)} %copy.9, bf16[1,8,512,640]{3,2,0,1:T(8,128)(2,1)} %all-gather.4.cloned.1.call-done, f32[8,512]{1,0:T(8,128)S(1)} %divide_select_fusion), kind=kOutput, calls=%fused_computation | convolution fusion | flops 13429637120 | bytes 32784384 | tf_op jit(solution)/shard_map/dot_general | solution.py:26
Async XLA Ops:
  6.5 53.1 %copy-start = (f32[32,8]{0,1:T(8,128)S(1)}, f32[32,8]{0,1:T(8,128)}, u32[]{:S(2)}) copy-start(f32[32,8]{0,1:T(8,128)} %param.7) | copy-start | bytes 3076
  6.5 187.9 %all-gather.6.cloned.1.call-start = ((), (), s32[]{:S(2)}) async-start(), calls=%async_computation.3 | async-start | bytes 21626880 | tf_op jit(solution)/shard_map/all_gather | solution.py:22
  25.5 207.7 %all-gather.4.cloned.1.call-start = ((), (), s32[]{:S(2)}) async-start(), calls=%async_computation.2 | async-start | bytes 5898240 | tf_op jit(solution)/shard_map/all_gather | solution.py:24
Sparse Core Ops, SparseCore 0:
  25.6 168.7 all-gather.5
  196.3 36.9 all-gather.3
where the time goes:
time: 264 us; the launch traced here: 263 us
  waiting for transfers between devices  142 us (54%)
  blocking collectives  50.3 us (19%)
  local copies, waits for them, and re-layouts  31.7 us (12%)
  matrix products  23.3 us (9%)
  between operations  14.1 us (5%)
    all_gather x1, waiting for transfers between devices, on_device(): rows_all = lax.all_gather(by_block, 'band', axis=3, tiled=True)[0]  134 us
    all_to_all x1, blocking collectives, on_device(): lax.all_to_all(pairs, 'band', split_axis=0, concat_axis=2, tiled=True)  32.6 us
    all_gather x1, local copies, waits for them, and re-layouts, on_device(): rows_all = lax.all_gather(by_block, 'band', axis=3, tiled=True)[0]  30.2 us
    dot_general x1, matrix products, on_device(): lax.dot_general(rows_all, scaled, (((1, 2), (0, 1)), ((), ())), preferred...  23.3 us
    all_to_all x1, blocking collectives, on_device(): lax.all_to_all(blocked, 'gvec', split_axis=0, concat_axis=2, tiled=True)  17.7 us
    all_gather x1, waiting for transfers between devices, on_device(): cols_all = lax.all_gather(by_column, 'gvec', axis=1, tiled=True)[0]  8.62 us
  transfers between devices with their start and end apart: 2, of which 2 were waited for; matrix products, arithmetic and copies ran while one was open for 12% of the time, Pallas kernels for 0%

commit v1 on v0

--- a/solution.py
+++ b/solution.py
@@ -20,7 +20,9 @@
     blocked = pairs.reshape(n_gvec, ratio, local_v, slot_count, col_width)
     by_block = lax.all_to_all(blocked, "gvec", split_axis=0, concat_axis=2, tiled=True)
     rows_all = lax.all_gather(by_block, "band", axis=3, tiled=True)[0]
-    by_column = lax.all_to_all(pairs, "band", split_axis=0, concat_axis=2, tiled=True)
+    shards = jnp.split(pairs, lax.axis_size("band"), axis=0)
+    received = lax.all_to_all(jnp.stack(shards), "band", 0, 0)
+    by_column = jnp.concatenate(received, axis=2)
     cols_all = lax.all_gather(by_column, "gvec", axis=1, tiled=True)[0]
     scaled = (weight[:, :, None] * cols_all.astype(jnp.float32)).astype(jnp.bfloat16)
     result = lax.dot_general(

time: 264 us -> 271 us (1.027)
  local copies, waits for them, and re-layouts: 31.7 us -> 55.2 us
  waiting for transfers between devices: 142 us -> 121 us
    unnamed x2 -> x33, local copies, waits for them, and re-layouts: 0.01 us -> 22.8 us
    all_gather x1, waiting for transfers between devices: 134 us -> 113 us  [on_device(): rows_all = lax.all_gather(by_block, 'band', axis=3, tiled=True)[0]]
  transfers between devices with their start and end apart: 2 -> 2, of which waited for: 2 -> 2; matrix products, arithmetic and copies ran while one was open for 12% -> 21% of each run, Pallas kernels for 0% -> 0%
where the time goes in v1:
time: 271 us; the launch traced here: 269 us
  waiting for transfers between devices  121 us (45%)
  local copies, waits for them, and re-layouts  55.2 us (20%)
  blocking collectives  52.9 us (20%)
  matrix products  23.3 us (9%)
  between operations  14.1 us (5%)
    all_gather x1, waiting for transfers between devices, on_device(): rows_all = lax.all_gather(by_block, 'band', axis=3, tiled=True)[0]  113 us
    all_to_all x1, blocking collectives, on_device(): received = lax.all_to_all(jnp.stack(shards), 'band', 0, 0)  35.2 us
    all_gather x1, local copies, waits for them, and re-layouts, on_device(): rows_all = lax.all_gather(by_block, 'band', axis=3, tiled=True)[0]  30.2 us
    dot_general x1, matrix products, on_device(): lax.dot_general(rows_all, scaled, (((1, 2), (0, 1)), ((), ())), preferred...  23.3 us
    unnamed x33, local copies, waits for them, and re-layouts  22.8 us
    all_to_all x1, blocking collectives, on_device(): lax.all_to_all(blocked, 'gvec', split_axis=0, concat_axis=2, tiled=True)  17.7 us
    all_gather x1, waiting for transfers between devices, on_device(): cols_all = lax.all_gather(by_column, 'gvec', axis=1, tiled=True)[0]  8.62 us
  transfers between devices with their start and end apart: 2, of which 2 were waited for; matrix products, arithmetic and copies ran while one was open for 21% of the time, Pallas kernels for 0%

profile of v1, /device:TPU:1, one launch (start us, length us, event | category | flops | bytes accessed | tf_op | source)
XLA Modules:
  0.0 268.5 jit_solution(13973692429775609040)
XLA Ops:
  6.5 17.7 %all_to_all.23 = bf16[8,4,1,16,640]{4,3,2,1,0:T(8,128)(2,1)S(1)} all-to-all(bf16[8,4,1,16,640]{4,3,2,1,0:T(8,128)(2,1)} %bitcast.90), channel_id=1, replica_groups=mesh['band'=32,'gvec'=8] {'gvec'}, dimensions={0} | all-to-all | bytes 1310720 | tf_op jit(solution)/shard_map/all_to_all | solution.py:21
  24.3 1.2 copy.8
  26.3 0.7 constant_dynamic-update-slice_fusion.30
  27.8 0.7 constant_dynamic-update-slice_fusion.28
  28.5 0.7 constant_dynamic-update-slice_fusion.27
  29.2 0.7 constant_dynamic-update-slice_fusion.26
  30.0 0.7 constant_dynamic-update-slice_fusion.25
  30.7 0.7 constant_dynamic-update-slice_fusion.24
  32.2 0.7 constant_dynamic-update-slice_fusion.22
  32.9 0.7 constant_dynamic-update-slice_fusion.21
  33.7 0.7 constant_dynamic-update-slice_fusion.20
  34.4 0.7 constant_dynamic-update-slice_fusion.19
  35.1 0.7 constant_dynamic-update-slice_fusion.18
  36.6 0.7 constant_dynamic-update-slice_fusion.16
  37.3 0.7 constant_dynamic-update-slice_fusion.15
  38.1 0.7 constant_dynamic-update-slice_fusion.14
  38.8 0.7 constant_dynamic-update-slice_fusion.13
  39.6 0.7 constant_dynamic-update-slice_fusion.12
  40.3 0.7 constant_dynamic-update-slice_fusion.11
  41.0 0.7 constant_dynamic-update-slice_fusion.10
  41.8 0.7 constant_dynamic-update-slice_fusion.9
  44.0 0.7 constant_dynamic-update-slice_fusion.6
  45.4 0.7 constant_dynamic-update-slice_fusion.4
  46.2 0.7 constant_dynamic-update-slice_fusion.3
  46.9 0.7 constant_dynamic-update-slice_fusion.2
  47.6 0.7 constant_dynamic-update-slice_fusion.1
  49.1 35.2 %all_to_all.24 = bf16[32,1,1,16,640]{4,3,2,1,0:T(8,128)(2,1)} all-to-all(bf16[32,1,1,16,640]{4,3,2,1,0:T(8,128)(2,1)S(1)} %constant_dynamic-update-slice_fusion), channel_id=1, replica_groups=mesh['band'=32,'gvec'=8] {'band'}, dimensions={0} | all-to-all | bytes 1310720 | tf_op jit(solution)/shard_map/all_to_all | solution.py:24
  86.0 0.8 divide_select_fusion
  86.8 112.8 %all-gather.6.cloned.1.call-done = bf16[1,4,8,1,512,640]{5,2,3,1,0,4:T(8,128)(2,1)} async-done(((bf16[1,4,8,1,16,640]{5,2,3,1,0,4:T(8,128)(2,1)}), bf16[1,4,8,1,512,640]{5,2,3,1,0,4:T(8,128)(2,1)}) %all-gather.6.cloned.1.call-update) | async-done | bytes 20971536 | tf_op jit(solution)/shard_map/all_gather | solution.py:22
  199.5 30.2 %copy.9 = bf16[1,4,8,1,512,640]{4,5,2,1,3,0:T(8,128)(2,1)} copy(bf16[1,4,8,1,512,640]{5,2,3,1,0,4:T(8,128)(2,1)} %all-gather.6.cloned.1.call-done) | data formatting | bytes 41943040 | tf_op jit(solution)/shard_map/all_gather | solution.py:22
  229.8 8.6 %all-gather.4.cloned.1.call-done = bf16[1,8,512,640]{3,2,0,1:T(8,128)(2,1)} async-done(((bf16[1,1,512,640]{3,2,0,1:T(8,128)(2,1)}), bf16[1,8,512,640]{3,2,0,1:T(8,128)(2,1)}) %all-gather.4.cloned.1.call-update) | async-done | bytes 5242896 | tf_op jit(solution)/shard_map/all_gather | solution.py:26
  238.4 23.3 %fusion = f32[640,4,640,1]{0,2,3,1:T(8,128)} fusion(bf16[1,4,8,1,512,640]{4,5,2,1,3,0:T(8,128)(2,1)} %copy.9, bf16[1,8,512,640]{3,2,0,1:T(8,128)(2,1)} %all-gather.4.cloned.1.call-done, f32[8,512]{1,0:T(8,128)S(1)} %divide_select_fusion), kind=kOutput, calls=%fused_computation | convolution fusion | flops 13429637120 | bytes 32784384 | tf_op jit(solution)/shard_map/dot_general | solution.py:28
  (17 shorter events, 7.0 us)
Async XLA Ops:
  6.5 79.3 %copy-start = (f32[32,8]{0,1:T(8,128)S(1)}, f32[32,8]{0,1:T(8,128)}, u32[]{:S(2)}) copy-start(f32[32,8]{0,1:T(8,128)} %param.7) | copy-start | bytes 3076
  6.5 193.0 %all-gather.6.cloned.1.call-start = ((), (), s32[]{:S(2)}) async-start(), calls=%async_computation.3 | async-start | bytes 21626880 | tf_op jit(solution)/shard_map/all_gather | solution.py:22
  25.5 212.9 %all-gather.4.cloned.1.call-start = ((), (), s32[]{:S(2)}) async-start(), calls=%async_computation.2 | async-start | bytes 5898240 | tf_op jit(solution)/shard_map/all_gather | solution.py:26
Sparse Core Ops, SparseCore 0:
  25.6 173.8 all-gather.5
  201.4 36.9 all-gather.3
